TPU v7x, 32 devices: a whole 2x2x4 slice. The times are simulated.
32 devices in a mesh: group: 2 (over x), expert: 8 (over z, y), attn: 2 (over core).
Axes of the slice: x: 2, y: 2, z: 4, core: 2. Of those that a mesh axis runs over, the one named last changes fastest.
Arguments:
- tokens: bfloat16 [4096, 7168], P(('group', 'expert', 'attn')), parts along dimension 0, may hold values from -6 to 6
- expert_ids: int32 [4096, 4], P(('group', 'expert', 'attn')), parts along dimension 0, may hold values from 0 to 7, all different within a row; in each aligned block of 128 rows (0 to 127, 128 to 255, ...) at most 80 rows name the same one
- gate_values: float32 [4096, 4], P(('group', 'expert', 'attn')), parts along dimension 0, may hold values from 0.1 to 1
- w_gate: bfloat16 [8, 7168, 1024], P('expert', None, 'attn'), may hold values from -0.0625 to 0.0625
- w_up: bfloat16 [8, 7168, 1024], P('expert', None, 'attn'), may hold values from -0.0625 to 0.0625
- w_down: bfloat16 [8, 1024, 7168], P('expert', 'attn'), may hold values from -0.1875 to 0.1875
Outputs:
- mixed_out: bfloat16 [4096, 7168], P(('group', 'expert', 'attn')), parts along dimension 0
There are 2 independent parts, one for each index of `group`. A program takes and returns all parts, laid end to end along the dimension named above; an argument that names none is the same for every part. Nothing has to cross between parts.
Inputs may be any that keep to these rules, and one draw needn't show every extreme that they name: `expert_ids`: each row names 4 different experts. Within the rows of one device no expert is named more than 80 times, a bound that some block reaches.
All inputs are finite; a program needn't handle non-finite values.
Results may differ from a plain program's by a relative error of at most 0.0065.
Values may be sent and summed in bfloat16 or wider, within the bound.
A program may use at most 128 MiB of HBM per device.

v0:
```python
import jax
import jax.numpy as jnp
from jax import lax
from jax.sharding import PartitionSpec as P


def shards(tokens, expert_ids, gate_values, w_gate, w_up, w_down):
    experts = lax.axis_size("expert")
    tok_rows = tokens.shape[0]
    top_count = expert_ids.shape[1]
    width = tokens.shape[1]
    capacity = (tok_rows * top_count * 5 // (4 * experts) + 7) // 8 * 8
    flat_ids = expert_ids.reshape(-1)
    onehot = (flat_ids[:, None] == jnp.arange(experts, dtype=jnp.int32)[None, :]).astype(jnp.int32)
    before = jnp.cumsum(onehot, axis=0) - onehot
    slot_index = jnp.sum(before * onehot, axis=1)
    position = flat_ids * capacity + slot_index
    placing = jnp.arange(experts * capacity, dtype=jnp.int32)[:, None] == position[None, :]
    placing = jnp.sum(
        placing.reshape(experts * capacity, tok_rows, top_count).astype(jnp.int32), axis=2
    ).astype(jnp.bfloat16)
    outgoing = jnp.dot(placing, tokens, preferred_element_type=jnp.float32).astype(jnp.bfloat16)
    outgoing = outgoing.reshape(experts, capacity, width)
    gate_proj = w_gate[0]
    up_proj = w_up[0]
    down_proj = w_down[0]
    paired = lax.all_gather(
        lax.all_to_all(outgoing, "expert", split_axis=0, concat_axis=0, tiled=True),
        "attn",
        axis=1,
        tiled=True,
    )
    flat_rows = paired.reshape(-1, width)
    gate_act = jnp.dot(flat_rows, gate_proj, preferred_element_type=jnp.float32)
    up_act = jnp.dot(flat_rows, up_proj, preferred_element_type=jnp.float32)
    hidden = (jax.nn.silu(gate_act) * up_act).astype(jnp.bfloat16)
    partial_value = (
        jnp.dot(hidden, down_proj, preferred_element_type=jnp.float32)
        .astype(jnp.bfloat16)
        .reshape(paired.shape)
    )
    summed = (
        lax.psum_scatter(partial_value, "attn", scatter_dimension=1, tiled=True)
        .astype(jnp.float32)
        .astype(jnp.bfloat16)
    )
    returned = lax.all_to_all(summed, "expert", split_axis=0, concat_axis=0, tiled=True)
    picked = returned.reshape(experts * capacity, width)[position]
    picked = picked.reshape(tok_rows, top_count, width)
    mixed_out = jnp.sum(picked.astype(jnp.float32) * gate_values[:, :, None], axis=1)
    return mixed_out.astype(jnp.bfloat16)


def solution(mesh):
    placed = (
        P(("group", "expert", "attn"), None),
        P(("group", "expert", "attn"), None),
        P(("group", "expert", "attn"), None),
        P("expert", None, "attn"),
        P("expert", None, "attn"),
        P("expert", "attn", None),
    )
    return jax.shard_map(
        shards,
        mesh=mesh,
        in_specs=placed,
        out_specs=P(("group", "expert", "attn"), None),
        check_vma=False,
    )
```

profile of v0, /device:TPU:0, one launch (start us, length us, event | category | flops | bytes accessed | tf_op | source)
XLA Modules:
  0.0 584.1 jit_solution(10683873261909486220)
XLA Ops:
  6.5 0.0 copy-start
  6.5 0.0 all-gather.2.cloned.1.call-start
  6.5 0.9 copy.13
  7.5 0.1 eq.44
  7.6 0.1 eq.40
  7.7 1.1 reduce-window.6
  8.8 0.2 slice_reduce_fusion
  9.1 0.1 fusion.13
  9.2 0.1 reduce_sum.32
  9.3 0.1 copy.16
  9.4 0.2 convert_reduce_fusion
  9.6 0.0 copy-done
  9.6 2.5 convolution_convert_fusion.1
  12.1 207.1 %all_to_all.10 = bf16[8,80,7168]{2,1,0:T(8,128)(2,1)} all-to-all(bf16[8,80,7168]{2,1,0:T(8,128)(2,1)S(1)} %bitcast.31), channel_id=1, replica_groups=mesh['group'=2,'expert'=8,'attn'=2] {'expert'}, dimensions={0} | all-to-all | bytes 18350080 | tf_op jit(solution)/shard_map/all_to_all | solution.py:28
  219.2 0.0 all-gather.2.cloned.1.call-update
  219.3 0.2 reduce-scatter.2.cloned.1.call-start
  219.5 30.9 %all-gather.2.cloned.1.call-done = bf16[8,160,7168]{2,1,0:T(8,128)(2,1)} async-done(((bf16[8,80,7168]{2,1,0:T(8,128)(2,1)}), bf16[8,160,7168]{2,1,0:T(8,128)(2,1)}) %all-gather.2.cloned.1.call-update) | async-done | bytes 18350096 | tf_op jit(solution)/shard_map/all_gather | solution.py:27
  250.3 0.0 copy-start.3
  250.3 16.7 %fusion.3 = f32[1280,512]{1,0:T(8,128)} fusion(bf16[1280,7168]{1,0:T(8,128)(2,1)} %bitcast.35, bf16[1,7168,512]{2,1,0:T(8,128)(2,1)} %param.9), kind=kOutput, calls=%fused_computation.7 | convolution fusion | flops 9395240960 | bytes 28311552 | tf_op jit(solution)/shard_map/dot_general | solution.py:34
  267.0 0.0 copy-done.3
  267.0 13.1 %fusion.8 = bf16[1280,512]{1,0:T(8,128)(2,1)S(1)} fusion(bf16[1280,7168]{1,0:T(8,128)(2,1)S(1)} %bitcast.36, bf16[1,7168,512]{2,1,0:T(8,128)(2,1)} %param.10, f32[1280,512]{1,0:T(8,128)} %fusion.3), kind=kOutput, calls=%fused_computation.10 | convolution fusion | flops 9399173120 | bytes 29622272 | tf_op jit(solution)/shard_map/dot_general | solution.py:35
  280.1 15.8 %convolution_convert_fusion = bf16[1280,7168]{1,0:T(8,128)(2,1)} fusion(bf16[1280,512]{1,0:T(8,128)(2,1)S(1)} %fusion.8, bf16[1,512,7168]{2,1,0:T(8,128)(2,1)} %param.11), kind=kOutput, calls=%fused_computation.1 | convolution fusion | flops 9404416000 | bytes 27000832 | tf_op jit(solution)/shard_map/dot_general | solution.py:38
  295.9 0.0 reduce-scatter.2.cloned.1.call-update
  295.9 0.0 copy-start.2
  295.9 29.0 %reduce-scatter.2.cloned.1.call-done = bf16[8,80,7168]{2,1,0:T(8,128)(2,1)} async-done(((bf16[8,160,7168]{2,1,0:T(8,128)(2,1)}), bf16[8,80,7168]{2,1,0:T(8,128)(2,1)}) %reduce-scatter.2.cloned.1.call-update) | async-done | bytes 9175056 | tf_op jit(solution)/shard_map/reduce_scatter | solution.py:43
  324.9 5.9 %all-to-all-start.1 = ((bf16[8,80,7168]{2,1,0:T(8,128)(2,1)}), bf16[8,80,7168]{2,1,0:T(8,128)(2,1)}, u32[]{:S(2)}, u32[]{:S(2)}) async-start(bf16[8,80,7168]{2,1,0:T(8,128)(2,1)} %reduce-scatter.2.cloned.1.call-done), calls=%async_computation.2 | async-start | bytes 18350080 | tf_op jit(solution)/shard_map/all_to_all | solution.py:47
  330.8 0.1 mul.43
  331.0 0.0 copy-done.2
  331.0 0.1 copy.17
  331.1 200.1 %all-to-all-done.1 = bf16[8,80,7168]{2,1,0:T(8,128)(2,1)} async-done(((bf16[8,80,7168]{2,1,0:T(8,128)(2,1)}), bf16[8,80,7168]{2,1,0:T(8,128)(2,1)}, u32[]{:S(2)}, u32[]{:S(2)}) %all-to-all-start.1) | async-done | bytes 9175072 | tf_op jit(solution)/shard_map/all_to_all | solution.py:47
  531.2 18.6 %gather_fusion = bf16[512,7168]{1,0:T(8,128)(2,1)} fusion(bf16[640,7168]{1,0:T(8,128)(2,1)} %bitcast.8, s32[1024]{0:T(1024)S(1)} %pad_clamp_fusion), kind=kCustom, calls=%fused_computation | custom fusion | bytes 14682112 | tf_op jit(solution)/shard_map/gather | solution.py:48
  549.8 0.0 copy-start.1
  549.8 14.1 %reshape.84 = f32[128,4,7168]{2,1,0:T(4,128)} reshape(bf16[512,7168]{1,0:T(8,128)(2,1)} %gather_fusion) | data formatting | bytes 22020096 | tf_op jit(solution)/shard_map/convert_element_type | solution.py:50
  563.8 13.5 %multiply_reduce_fusion = bf16[128,7168]{1,0:T(8,128)(2,1)} fusion(f32[128,4,7168]{2,1,0:T(4,128)} %reshape.84, f32[128,4]{1,0:T(8,128)S(1)} %copy.17), kind=kLoop, calls=%fused_computation.2 | loop fusion | flops 6422528 | bytes 16517120 | tf_op jit(solution)/shard_map/reduce_sum | solution.py:50
  577.3 0.0 copy-done.1
  (6 shorter events, 0.1 us)
Async XLA Ops:
  6.5 3.0 copy-start
  6.5 243.8 %all-gather.2.cloned.1.call-start = ((), (), s32[]{:S(2)}) async-start(), calls=%async_computation.3 | async-start | bytes 27525120 | tf_op jit(solution)/shard_map/all_gather | solution.py:27
  219.3 105.7 %reduce-scatter.2.cloned.1.call-start = ((), (), s32[]{:S(2)}) async-start(), calls=%async_computation.4 | async-start | bytes 27525120 | tf_op jit(solution)/shard_map/reduce_scatter | solution.py:43
  250.3 16.7 %copy-start.3 = (bf16[8,160,7168]{2,1,0:T(8,128)(2,1)S(1)}, bf16[8,160,7168]{2,1,0:T(8,128)(2,1)}, u32[]{:S(2)}) copy-start(bf16[8,160,7168]{2,1,0:T(8,128)(2,1)} %all-gather.2.cloned.1.call-done) | copy-start | bytes 55050244
  295.9 35.0 %copy-start.2 = (f32[128,4]{0,1:T(4,128)S(1)}, f32[128,4]{0,1:T(4,128)}, u32[]{:S(2)}) copy-start(f32[128,4]{0,1:T(4,128)} %param.8) | copy-start | bytes 6148
  324.9 206.3 %all-to-all-start.1 = ((bf16[8,80,7168]{2,1,0:T(8,128)(2,1)}), bf16[8,80,7168]{2,1,0:T(8,128)(2,1)}, u32[]{:S(2)}, u32[]{:S(2)}) async-start(bf16[8,80,7168]{2,1,0:T(8,128)(2,1)} %reduce-scatter.2.cloned.1.call-done), calls=%async_computation.2 | async-start | bytes 18350080 | tf_op jit(solution)/shard_map/all_to_all | solution.py:47
  549.8 27.5 %copy-start.1 = (bf16[128,7168]{1,0:T(8,128)(2,1)S(1)}, bf16[128,7168]{1,0:T(8,128)(2,1)}, u32[]{:S(2)}) copy-start(bf16[128,7168]{1,0:T(8,128)(2,1)} %param.6) | copy-start | bytes 5505028
Sparse Core Ops, SparseCore 0:
  219.4 30.9 all-gather.1
  296.1 28.8 reduce-scatter.1
where the time goes:
time: 585 us; the launch traced here: 584 us
  waiting for transfers between devices  260 us (44%)
  blocking collectives  207 us (35%)
  matrix products  48.1 us (8%)
  local copies, waits for them, and re-layouts  34.4 us (6%)
  other arithmetic  15 us (3%)
  between operations  13.5 us (2%)
  starting transfers between devices  6.17 us (1%)
    all_to_all x1, blocking collectives, shards(): lax.all_to_all(outgoing, 'expert', split_axis=0, concat_axis=0, tiled=True)  207 us
    all_to_all x1, waiting for transfers between devices, shards(): lax.all_to_all(summed, 'expert', split_axis=0, concat_axis=0, tiled=True)  200 us
    all_gather x1, waiting for transfers between devices, shards(): lax.all_gather(lax.all_to_all(outgoing, 'expert', split_axis=0, concat_ax...  30.9 us
    reduce_scatter x1, waiting for transfers between devices, shards(): lax.psum_scatter(partial_value, 'attn', scatter_dimension=1, tiled=True)  29 us
    gather x1, local copies, waits for them, and re-layouts, shards(): picked = returned.reshape(experts * capacity, width)[position]  18.6 us
    dot_general x1, matrix products, shards(): gate_act = jnp.dot(flat_rows, gate_proj, preferred_element_type=jnp.float32)  16.7 us
    dot_general x1, matrix products, shards(): jnp.dot(hidden, down_proj, preferred_element_type=jnp.float32)  15.8 us
    convert_element_type x1, local copies, waits for them, and re-layouts, shards(): picked.astype(jnp.float32) * gate_values[:, :, None]  14.1 us
  transfers between devices with their start and end apart: 3, of which 3 were waited for; matrix products, arithmetic and copies ran while one was open for 0% of the time, Pallas kernels for 0%

commit v1 on v0

v1 whole, which is shorter than its diff:
```python
import jax
import jax.numpy as jnp
from jax import lax
from jax.sharding import PartitionSpec as P


def shards(tokens, expert_ids, gate_values, w_gate, w_up, w_down):
    experts = lax.axis_size("expert")
    chosen = expert_ids[:, :, None] == jnp.arange(experts, dtype=jnp.int32)[None, None, :]
    weight = jnp.sum(jnp.where(chosen, gate_values[:, :, None], 0.0), axis=1)
    weights = lax.all_gather(weight, ("expert", "attn"), axis=0, tiled=True)
    mine = lax.dynamic_index_in_dim(weights, lax.axis_index("expert"), 1, keepdims=True)
    rows = lax.all_gather(tokens, ("expert", "attn"), axis=0, tiled=True)
    gate_act = jnp.dot(rows, w_gate[0], preferred_element_type=jnp.float32)
    up_act = jnp.dot(rows, w_up[0], preferred_element_type=jnp.float32)
    hidden = (jax.nn.silu(gate_act) * up_act * mine).astype(jnp.bfloat16)
    partial_value = jnp.dot(hidden, w_down[0], preferred_element_type=jnp.float32).astype(jnp.bfloat16)
    return lax.psum_scatter(partial_value, ("expert", "attn"), scatter_dimension=0, tiled=True)


def solution(mesh):
    placed = (
        P(("group", "expert", "attn"), None),
        P(("group", "expert", "attn"), None),
        P(("group", "expert", "attn"), None),
        P("expert", None, "attn"),
        P("expert", None, "attn"),
        P("expert", "attn", None),
    )
    return jax.shard_map(
        shards,
        mesh=mesh,
        in_specs=placed,
        out_specs=P(("group", "expert", "attn"), None),
        check_vma=False,
    )
```

time: 585 us -> 510 us (0.87)
  blocking collectives: 207 us -> 23.6 us
  waiting for transfers between devices: 260 us -> 407 us
  local copies, waits for them, and re-layouts: 34.4 us -> 0.01 us
  matrix products: 48.1 us -> 65.5 us
  other arithmetic: 15 us -> 0.71 us
  starting transfers between devices: 6.17 us -> 0.04 us
    reduce_scatter x1, waiting for transfers between devices: 29 us -> 278 us  [shards(): lax.psum_scatter(partial_value, ('expert', 'attn'), scatter_dimension=0,...]
    all_to_all x1 -> x0, blocking collectives: 207 us -> none  [shards(): lax.all_to_all(outgoing, 'expert', split_axis=0, concat_axis=0, tiled=True)]
    all_to_all x1 -> x0, waiting for transfers between devices: 200 us -> none  [shards(): lax.all_to_all(summed, 'expert', split_axis=0, concat_axis=0, tiled=True)]
    all_gather x1, waiting for transfers between devices: 30.9 us -> 128 us  [shards(): rows = lax.all_gather(tokens, ('expert', 'attn'), axis=0, tiled=True)]
    all_gather x0 -> x1, blocking collectives: none -> 23.6 us  [shards(): weights = lax.all_gather(weight, ('expert', 'attn'), axis=0, tiled=True)]
    gather x1 -> x0, local copies, waits for them, and re-layouts: 18.6 us -> none  [shards(): picked = returned.reshape(experts * capacity, width)[position]]
    dot_general x4 -> x3, matrix products: 48.1 us -> 65.5 us  [the longest x1 22.4 us: shards(): gate_act = jnp.dot(rows, w_gate[0], preferred_element_type=jnp.float32)]
    convert_element_type x1 -> x0, local copies, waits for them, and re-layouts: 14.1 us -> none  [shards(): picked.astype(jnp.float32) * gate_values[:, :, None]]
  transfers between devices with their start and end apart: 3 -> 2, of which waited for: 3 -> 2; matrix products, arithmetic and copies ran while one was open for 0% -> 0% of each run, Pallas kernels for 0% -> 0%
where the time goes in v1:
time: 510 us
  waiting for transfers between devices  407 us (80%)
  matrix products  65.5 us (13%)
  blocking collectives  23.6 us (5%)
  between operations  13.4 us (3%)
    reduce_scatter x1, waiting for transfers between devices, shards(): lax.psum_scatter(partial_value, ('expert', 'attn'), scatter_dimension=0,...  278 us
    all_gather x1, waiting for transfers between devices, shards(): rows = lax.all_gather(tokens, ('expert', 'attn'), axis=0, tiled=True)  128 us
    all_gather x1, blocking collectives, shards(): weights = lax.all_gather(weight, ('expert', 'attn'), axis=0, tiled=True)  23.6 us
    dot_general x1, matrix products, shards(): gate_act = jnp.dot(rows, w_gate[0], preferred_element_type=jnp.float32)  22.4 us
    dot_general x1, matrix products, shards(): jnp.dot(hidden, w_down[0], preferred_element_type=jnp.float32)  22.1 us
    dot_general x1, matrix products, shards(): up_act = jnp.dot(rows, w_up[0], preferred_element_type=jnp.float32)  21 us
  transfers between devices with their start and end apart: 2, of which 2 were waited for; matrix products, arithmetic and copies ran while one was open for 0% of the time, Pallas kernels for 0%

profile of v1, /device:TPU:0, one launch (start us, length us, event | category | flops | bytes accessed | tf_op | source)
XLA Modules:
  0.0 510.1 jit_solution(4122599244534441534)
XLA Ops:
  6.5 0.0 all-gather.2.cloned.1.call-start
  6.5 0.7 all-gather.2.cloned.1.call-update
  7.3 0.0 reduce-scatter.2.cloned.1.call-start
  7.3 0.7 select_reduce_fusion
  8.0 23.6 %all_gather.7 = f32[2048,8]{0,1:T(8,128)S(1)} all-gather(f32[128,8]{0,1:T(8,128)S(1)} %select_reduce_fusion), channel_id=1, replica_groups=mesh['group'=2,'expert'=8,'attn'=2] {'expert','attn'}, dimensions={0}, use_global_device_ids=true | all-gather | bytes 69632 | tf_op jit(solution)/shard_map/all_gather | solution.py:11
  31.6 128.5 %all-gather.2.cloned.1.call-done = bf16[2048,7168]{1,0:T(8,128)(2,1)} async-done(((bf16[128,7168]{1,0:T(8,128)(2,1)}), bf16[2048,7168]{1,0:T(8,128)(2,1)}) %all-gather.2.cloned.1.call-update) | async-done | bytes 29360144 | tf_op jit(solution)/shard_map/all_gather | solution.py:13
  160.1 21.0 %fusion.1 = f32[2048,512]{1,0:T(8,128)S(1)} fusion(bf16[2048,7168]{1,0:T(8,128)(2,1)} %all-gather.2.cloned.1.call-done, bf16[1,7168,512]{2,1,0:T(8,128)(2,1)} %param.10), kind=kOutput, calls=%fused_computation.2 | convolution fusion | flops 15032385536 | bytes 40894464 | tf_op jit(solution)/shard_map/dot_general | solution.py:15
  181.1 22.4 %multiply_convert_fusion = bf16[2048,512]{1,0:T(8,128)(2,1)S(1)} fusion(f32[2048,512]{1,0:T(8,128)S(1)} %fusion.1, bf16[2048,7168]{1,0:T(8,128)(2,1)} %all-gather.2.cloned.1.call-done, bf16[1,7168,512]{2,1,0:T(8,128)(2,1)} %param.9, f32[2048]{0:T(1024)S(1)} %bitcast.15), kind=kOutput, calls=%fused_computation.6 | convolution fusion | flops 15039725568 | bytes 42999808 | tf_op jit(solution)/shard_map/dot_general | solution.py:14
  203.5 22.1 %convolution_convert_fusion = bf16[2048,7168]{1,0:T(8,128)(2,1)} fusion(bf16[2048,512]{1,0:T(8,128)(2,1)S(1)} %multiply_convert_fusion, bf16[1,512,7168]{2,1,0:T(8,128)(2,1)} %param.11), kind=kOutput, calls=%fused_computation | convolution fusion | flops 15047065600 | bytes 38797312 | tf_op jit(solution)/shard_map/dot_general | solution.py:17
  225.6 0.0 reduce-scatter.2.cloned.1.call-update
  225.6 277.7 %reduce-scatter.2.cloned.1.call-done = bf16[128,7168]{1,0:T(8,128)(2,1)} async-done(((bf16[2048,7168]{1,0:T(8,128)(2,1)}), bf16[128,7168]{1,0:T(8,128)(2,1)}) %reduce-scatter.2.cloned.1.call-update) | async-done | bytes 1835024 | tf_op jit(solution)/shard_map/reduce_scatter | solution.py:18
  (1 shorter events, 0.0 us)
Async XLA Ops:
  6.5 153.5 %all-gather.2.cloned.1.call-start = ((), (), s32[]{:S(2)}) async-start(), calls=%async_computation.1 | async-start | bytes 31195136 | tf_op jit(solution)/shard_map/all_gather | solution.py:13
  7.3 496.0 %reduce-scatter.2.cloned.1.call-start = ((), (), s32[]{:S(2)}) async-start(), calls=%async_computation.2 | async-start | bytes 31195136 | tf_op jit(solution)/shard_map/reduce_scatter | solution.py:18
Sparse Core Ops, SparseCore 0:
  9.0 151.0 all-gather.1
  225.7 277.5 reduce-scatter.1

commit v2 on v0

--- a/solution.py
+++ b/solution.py
@@ -1,7 +1,269 @@
+import functools
 import jax
 import jax.numpy as jnp
 from jax import lax
+from jax.experimental import pallas as pl
+from jax.experimental.pallas import tpu as pltpu
 from jax.sharding import PartitionSpec as P
+
+MESH = pl.DeviceIdType.MESH
+SUBS = 2
+TILE = 256
+
+
+def ring_kernel(experts, x_ref, wt_ref, wg_ref, wu_ref, wd_ref, out_ref, sib_ref,
+                gates, ups, own, held, far, own_wt, held_wt, far_wt,
+                hid_own, hid, hid_far, first_out, first_in, second_out,
+                load_sem, sib_send, sib_recv, ag_send, ag_recv, wt_send, wt_recv,
+                far_send, far_recv, rs_send, rs_recv, down_sem):
+    half = experts // 2
+    rows, width = x_ref.shape
+    units = wg_ref.shape[1]
+    part = width // SUBS
+    mid = rows // 2
+    me = lax.axis_index("expert")
+    core = lax.axis_index("attn")
+
+    def owner_at(pos):
+        turn = pos // half
+        line = pos + turn * (experts - 1 - 2 * pos)
+        return 2 * line + turn
+
+    line, turn = me // 2, me % 2
+    pos = line + turn * (experts - 1 - 2 * line)
+    right = {"expert": owner_at((pos + 1) % experts)}
+    left = {"expert": owner_at((pos + experts - 1) % experts)}
+    other = {"attn": 1 - core}
+
+    barrier = pltpu.get_barrier_semaphore()
+    for peer in (left, right, other):
+        pl.semaphore_signal(barrier, inc=1, device_id=peer, device_id_type=MESH)
+    pl.semaphore_wait(barrier, 3)
+
+    def remote(src, dst, send, recv, peer):
+        return pltpu.make_async_remote_copy(
+            src_ref=src, dst_ref=dst, send_sem=send, recv_sem=recv,
+            device_id=peer, device_id_type=MESH)
+
+    def side_rows(side):
+        return pl.ds(side * rows, rows)
+
+    def gather_copies(dist):
+        copies = []
+        for side, peer in ((0, right), (1, left)):
+            for j in range(SUBS):
+                if dist == 1:
+                    src = x_ref.at[:, pl.ds(j * part, part)]
+                else:
+                    src = held.at[dist - 2, j, side_rows(side)]
+                copies.append(remote(src, held.at[dist - 1, j, side_rows(side)],
+                                     ag_send.at[dist - 1, side, j], ag_recv.at[dist - 1, side, j], peer))
+            wsrc = wt_ref if dist == 1 else held_wt.at[dist - 2, side]
+            copies.append(remote(wsrc, held_wt.at[dist - 1, side],
+                                 wt_send.at[dist - 1, side], wt_recv.at[dist - 1, side], peer))
+        return copies
+
+    def far_copies():
+        copies = []
+        for side, peer in ((0, right), (1, left)):
+            for j in range(SUBS):
+                copies.append(remote(held.at[half - 2, j, pl.ds(side * rows + side * mid, mid)],
+                                     far.at[j, pl.ds(side * mid, mid)],
+                                     far_send.at[side, j], far_recv.at[side, j], peer))
+        copies.append(remote(held_wt.at[half - 2, 0], far_wt, wt_send.at[half - 1, 0],
+                             wt_recv.at[half - 1, 0], right))
+        return copies
+
+    hops = [gather_copies(dist) for dist in range(1, half)] + [far_copies()]
+    for copy in hops[0]:
+        copy.start()
+
+    loads = [pltpu.make_async_copy(wg_ref, gates.at[core], load_sem.at[0]),
+             pltpu.make_async_copy(wu_ref, ups.at[core], load_sem.at[1]),
+             pltpu.make_async_copy(wt_ref, own_wt, load_sem.at[2])]
+    for j in range(SUBS):
+        loads.append(pltpu.make_async_copy(x_ref.at[:, pl.ds(j * part, part)], own.at[j], load_sem.at[3 + j]))
+    swaps = [remote(wg_ref, gates.at[core], sib_send.at[0], sib_recv.at[0], other),
+             remote(wu_ref, ups.at[core], sib_send.at[1], sib_recv.at[1], other),
+             remote(wd_ref, sib_ref, sib_send.at[2], sib_recv.at[2], other)]
+    for copy in loads + swaps:
+        copy.start()
+
+    def column(table):
+        names = lax.broadcasted_iota(jnp.int32, table.shape, 0)
+        line_of = jnp.sum(jnp.where(names == me, table, 0.0), axis=0, keepdims=True)
+        square = (rows, rows)
+        same = lax.broadcasted_iota(jnp.int32, square, 0) == lax.broadcasted_iota(jnp.int32, square, 1)
+        return jnp.sum(jnp.where(same, jnp.broadcast_to(line_of, square), 0.0), axis=1, keepdims=True)
+
+    def expand(chunks, weight, target):
+        def one(q, carry):
+            r, n = q // (units // TILE), q % (units // TILE)
+            cols = pl.ds(pl.multiple_of(n * TILE, TILE), TILE)
+            gate_act = jnp.zeros((weight.shape[0], TILE), jnp.float32)
+            up_act = gate_act
+            for j, chunk in enumerate(chunks):
+                deep = pl.ds(j * part, part)
+                gate_act += jnp.dot(chunk[...], gates[r, deep, cols], preferred_element_type=jnp.float32)
+                up_act += jnp.dot(chunk[...], ups[r, deep, cols], preferred_element_type=jnp.float32)
+            value = gate_act / (1.0 + jnp.exp(-gate_act)) * up_act * weight
+            target[:, pl.ds(pl.multiple_of(q * TILE, TILE), TILE)] = value.astype(jnp.bfloat16)
+            return carry
+
+        lax.fori_loop(0, 2 * units // TILE, one, 0)
+
+    for dist in range(1, half):
+        for copy in hops[dist - 1]:
+            copy.wait_recv()
+        for copy in hops[dist]:
+            copy.start()
+        if dist == 1:
+            for copy in loads:
+                copy.wait()
+            for copy in swaps[:2]:
+                copy.wait()
+            expand([own.at[j] for j in range(SUBS)], column(own_wt[...]), hid_own)
+        weight = jnp.concatenate([column(held_wt[dist - 1, 0]), column(held_wt[dist - 1, 1])], axis=0)
+        expand([held.at[dist - 1, j] for j in range(SUBS)], weight, hid.at[dist - 1])
+    swaps[2].wait()
+    for copy in hops[half - 1]:
+        copy.wait_recv()
+    expand([far.at[j] for j in range(SUBS)], column(far_wt[...]), hid_far)
+    for hop in hops:
+        for copy in hop:
+            copy.wait_send()
+
+    blocks = width // units
+
+    def down_copy(r, b):
+        place = pl.ds(pl.multiple_of(b * units, units), units)
+        return [pltpu.make_async_copy(wd_ref.at[:, place], gates.at[core, place], down_sem.at[0, b]),
+                pltpu.make_async_copy(sib_ref.at[:, place], gates.at[1 - core, place], down_sem.at[1, b])]
+
+    def start_down(b, carry):
+        for copy in down_copy(0, b):
+            copy.start()
+        return carry
+
+    def wait_down(b, carry):
+        for copy in down_copy(0, b):
+            copy.wait()
+        return carry
+
+    lax.fori_loop(0, blocks, start_down, 0)
+    lax.fori_loop(0, blocks, wait_down, 0)
+
+    def contract(j, hidden, write):
+        def one(t, carry):
+            place = pl.ds(pl.multiple_of((j * (part // units) + t) * units, units), units)
+            total = jnp.dot(hidden[:, :units], gates[0, place, :], preferred_element_type=jnp.float32)
+            total += jnp.dot(hidden[:, units:], gates[1, place, :], preferred_element_type=jnp.float32)
+            write(pl.ds(pl.multiple_of(t * units, units), units), total)
+            return carry
+
+        lax.fori_loop(0, part // units, one, 0)
+
+    sums = {}
+    for j in range(SUBS):
+        def write(cols, total, j=j):
+            first_out[j, :, cols] = total.astype(jnp.bfloat16)
+
+        contract(j, hid_far, write)
+        pair = []
+        for side, peer in ((0, left), (1, right)):
+            piece = pl.ds((1 - side) * mid, mid)
+            pair.append(remote(first_out.at[j, piece], first_in.at[j, piece],
+                               rs_send.at[0, side, j], rs_recv.at[0, side, j], peer))
+        for copy in pair:
+            copy.start()
+        sums[0, j] = pair
+    for k in range(1, half):
+        dist = half - k
+        for j in range(SUBS):
+            for copy in sums[k - 1, j]:
+                copy.wait_recv()
+            if k == 1:
+                source = second_out.at[j]
+
+                def write(cols, total, j=j):
+                    second_out[j, :mid, cols] = total[:mid].astype(jnp.bfloat16)
+                    second_out[j, mid:rows, cols] = (
+                        total[mid:rows] + first_in[j, mid:, cols].astype(jnp.float32)).astype(jnp.bfloat16)
+                    second_out[j, rows:rows + mid, cols] = (
+                        total[rows:rows + mid] + first_in[j, :mid, cols].astype(jnp.float32)).astype(jnp.bfloat16)
+                    second_out[j, rows + mid:, cols] = total[rows + mid:].astype(jnp.bfloat16)
+            else:
+                source = held.at[k - 2, j]
+
+                def write(cols, total, k=k, j=j):
+                    held[k - 2, j, :, cols] = (
+                        total + held[k - 2, j, :, cols].astype(jnp.float32)).astype(jnp.bfloat16)
+
+            contract(j, hid.at[dist - 1], write)
+            pair = []
+            for side, peer in ((0, left), (1, right)):
+                pair.append(remote(source.at[side_rows(side)], held.at[k - 1, j, side_rows(side)],
+                                   rs_send.at[k, side, j], rs_recv.at[k, side, j], peer))
+            for copy in pair:
+                copy.start()
+            sums[k, j] = pair
+    for j in range(SUBS):
+        for copy in sums[half - 1, j]:
+            copy.wait_recv()
+
+        def write(cols, total, j=j):
+            both = held[half - 2, j, :rows, cols].astype(jnp.float32) + held[half - 2, j, rows:, cols].astype(jnp.float32)
+            own[j, :, cols] = (total + both).astype(jnp.bfloat16)
+
+        contract(j, hid_own, write)
+        out_ref[:, j * part:(j + 1) * part] = own[j]
+    for pair in sums.values():
+        for copy in pair:
+            copy.wait_send()
+
+
+def ring_shards(tokens, expert_ids, gate_values, w_gate, w_up, w_down):
+    experts = lax.axis_size("expert")
+    rows, width = tokens.shape
+    units = w_gate.shape[2]
+    half = experts // 2
+    chosen = expert_ids.T[:, None, :] == jnp.arange(experts, dtype=jnp.int32)[None, :, None]
+    table = jnp.sum(jnp.where(chosen, gate_values.T[:, None, :], 0.0), axis=0)
+    part = width // SUBS
+    bf, f32 = jnp.bfloat16, jnp.float32
+    dma = pltpu.SemaphoreType.DMA
+    anywhere = pl.BlockSpec(memory_space=pl.ANY)
+    out, _ = pl.pallas_call(
+        functools.partial(ring_kernel, experts),
+        out_shape=(jax.ShapeDtypeStruct((rows, width), bf), jax.ShapeDtypeStruct((units, width), bf)),
+        in_specs=[anywhere] * 5,
+        out_specs=(pl.BlockSpec(memory_space=pltpu.VMEM), anywhere),
+        scratch_shapes=[
+            pltpu.VMEM((2, width, units), bf),
+            pltpu.VMEM((2, width, units), bf),
+            pltpu.VMEM((SUBS, rows, part), bf),
+            pltpu.VMEM((half - 1, SUBS, 2 * rows, part), bf),
+            pltpu.VMEM((SUBS, rows, part), bf),
+            pltpu.VMEM((experts, rows), f32),
+            pltpu.VMEM((half - 1, 2, experts, rows), f32),
+            pltpu.VMEM((experts, rows), f32),
+            pltpu.VMEM((rows, 2 * units), bf),
+            pltpu.VMEM((half - 1, 2 * rows, 2 * units), bf),
+            pltpu.VMEM((rows, 2 * units), bf),
+            pltpu.VMEM((SUBS, rows, part), bf),
+            pltpu.VMEM((SUBS, rows, part), bf),
+            pltpu.VMEM((SUBS, 2 * rows, part), bf),
+            dma((3 + SUBS,)), dma((3,)), dma((3,)),
+            dma((half - 1, 2, SUBS)), dma((half - 1, 2, SUBS)),
+            dma((half, 2)), dma((half, 2)),
+            dma((2, SUBS)), dma((2, SUBS)),
+            dma((half, 2, SUBS)), dma((half, 2, SUBS)),
+            dma((2, width // units)),
+        ],
+        compiler_params=pltpu.CompilerParams(
+            collective_id=0, has_side_effects=True, vmem_limit_bytes=60 * 2 ** 20),
+    )(tokens, table, w_gate[0], w_up[0], w_down[0])
+    return out
 
 
 def shards(tokens, expert_ids, gate_values, w_gate, w_up, w_down):
@@ -60,10 +322,19 @@
         P("expert", None, "attn"),
         P("expert", "attn", None),
     )
-    return jax.shard_map(
-        shards,
-        mesh=mesh,
-        in_specs=placed,
-        out_specs=P(("group", "expert", "attn"), None),
-        check_vma=False,
-    )
+
+    def run(tokens, expert_ids, gate_values, w_gate, w_up, w_down):
+        experts, cores = mesh.shape["expert"], mesh.shape["attn"]
+        block = tokens.size * 2 // mesh.size
+        weights = w_gate.size * 2 // experts
+        need = block * (experts + 7) + 2 * weights
+        fits = cores == 2 and experts % 2 == 0 and experts >= 4 and need <= 58 * 2 ** 20
+        return jax.shard_map(
+            ring_shards if fits else shards,
+            mesh=mesh,
+            in_specs=placed,
+            out_specs=P(("group", "expert", "attn"), None),
+            check_vma=False,
+        )(tokens, expert_ids, gate_values, w_gate, w_up, w_down)
+
+    return run

time: 585 us -> 305 us (0.52)
  Pallas kernels: 0 us -> 301 us
  waiting for transfers between devices: 260 us -> 0 us
  blocking collectives: 207 us -> 0 us
  matrix products: 48.1 us -> 0 us
  local copies, waits for them, and re-layouts: 34.4 us -> 2.85 us
  other arithmetic: 15 us -> 1.3 us
  between operations: 13.5 us -> 0.01 us
  starting transfers between devices: 6.17 us -> 0 us
    pallas_call x0 -> x1, Pallas kernels: none -> 301 us  [ring_shards(): pl.pallas_call(functools.partial(ring_kernel, experts), out_shape=(jax.Sh...]
    all_to_all x1 -> x0, blocking collectives: 207 us -> none  [shards(): lax.all_to_all(outgoing, 'expert', split_axis=0, concat_axis=0, tiled=True)]
    all_to_all x1 -> x0, waiting for transfers between devices: 200 us -> none  [shards(): lax.all_to_all(summed, 'expert', split_axis=0, concat_axis=0, tiled=True)]
    dot_general x4 -> x0, matrix products: 48.1 us -> none  [the longest x1 16.7 us: shards(): gate_act = jnp.dot(flat_rows, gate_proj, preferred_element_type=jnp.float32)]
    all_gather x1 -> x0, waiting for transfers between devices: 30.9 us -> none  [shards(): lax.all_gather(lax.all_to_all(outgoing, 'expert', split_axis=0, concat_ax...]
    reduce_scatter x1 -> x0, waiting for transfers between devices: 29 us -> none  [shards(): lax.psum_scatter(partial_value, 'attn', scatter_dimension=1, tiled=True)]
    gather x1 -> x0, local copies, waits for them, and re-layouts: 18.6 us -> none  [shards(): picked = returned.reshape(experts * capacity, width)[position]]
    convert_element_type x1 -> x0, local copies, waits for them, and re-layouts: 14.1 us -> none  [shards(): picked.astype(jnp.float32) * gate_values[:, :, None]]
  transfers between devices with their start and end apart: 3 -> 0, of which waited for: 3 -> 0; matrix products, arithmetic and copies ran while one was open for 0% -> 0% of each run, Pallas kernels for 0% -> 0%
where the time goes in v2:
time: 305 us
  Pallas kernels  301 us (99%)
    pallas_call x1, Pallas kernels, ring_shards(): pl.pallas_call(functools.partial(ring_kernel, experts), out_shape=(jax.Sh...  301 us

profile of v2, /device:TPU:0, one launch (start us, length us, event | category | flops | bytes accessed | tf_op | source)
XLA Modules:
  0.0 305.2 jit_solution(13740462983516783327)
XLA Ops:
  0.0 1.3 select_reduce_fusion.wt_ref
  1.3 301.1 %shard_map.64 = (bf16[128,7168]{1,0:T(8,128)(2,1)}, bf16[512,7168]{1,0:T(8,128)(2,1)}) custom-call(bf16[128,7168]{1,0:T(8,128)(2,1)} %x_ref.1, f32[8,128]{1,0:T(8,128)} %select_reduce_fusion.wt_ref, bf16[7168,512]{1,0:T(8,128)(2,1)} %bitcast.5, bf16[7168,512]{1,0:T(8,128)(2,1)} %bitcast.6, bf16[512,7168]{1,0:T(8,128)(2,1)} %bitcast.7), custom_call_target="tpu_custom_call" | custom-call | tf_op jit(solution)/shard_map/pallas_call | solution.py:236
  302.4 2.8 copy.8

commit v3 on v2

--- a/solution.py
+++ b/solution.py
@@ -12,15 +12,15 @@
 
 
 def ring_kernel(experts, x_ref, wt_ref, wg_ref, wu_ref, wd_ref, out_ref, sib_ref,
-                gates, ups, own, held, far, own_wt, held_wt, far_wt,
-                hid_own, hid, hid_far, first_out, first_in, second_out,
+                gates, ups, own, held, late, far, own_wt, held_wt, far_wt,
+                hid_own, hid, hid_late, hid_far, hid_wide, stage, stage_far, first_in, late_in, second_out,
                 load_sem, sib_send, sib_recv, ag_send, ag_recv, wt_send, wt_recv,
-                far_send, far_recv, rs_send, rs_recv, down_sem):
+                rs_send, rs_recv, down_sem):
     half = experts // 2
     rows, width = x_ref.shape
     units = wg_ref.shape[1]
     part = width // SUBS
-    mid = rows // 2
+    cap = far.shape[1]
     me = lax.axis_index("expert")
     core = lax.axis_index("attn")
 
@@ -31,8 +31,9 @@
 
     line, turn = me // 2, me % 2
     pos = line + turn * (experts - 1 - 2 * line)
-    right = {"expert": owner_at((pos + 1) % experts)}
-    left = {"expert": owner_at((pos + experts - 1) % experts)}
+    right_owner = owner_at((pos + 1) % experts)
+    left_owner = owner_at((pos + experts - 1) % experts)
+    right, left = {"expert": right_owner}, {"expert": left_owner}
     other = {"attn": 1 - core}
 
     barrier = pltpu.get_barrier_semaphore()
@@ -45,38 +46,42 @@
             src_ref=src, dst_ref=dst, send_sem=send, recv_sem=recv,
             device_id=peer, device_id_type=MESH)
 
+    ahead = ((right, right_owner), (left, left_owner))
+
     def side_rows(side):
         return pl.ds(side * rows, rows)
 
-    def gather_copies(dist):
-        copies = []
-        for side, peer in ((0, right), (1, left)):
+    def cap_rows(side):
+        return pl.ds(side * cap, cap)
+
+    def hop_copy(dist, side, j):
+        if dist == half:
+            src, dst = stage_far.at[side], far.at[j]
+        elif dist == half - 1 and j != side:
+            src, dst = stage.at[side], late.at[j, cap_rows(side)]
+        else:
+            src = x_ref.at[:, pl.ds(j * part, part)] if dist == 1 else held.at[dist - 2, j, side_rows(side)]
+            dst = held.at[dist - 1, j, side_rows(side)]
+        return remote(src, dst, ag_send.at[dist - 1, side, j], ag_recv.at[dist - 1, side, j], ahead[side][0])
+
+    def table_copy(dist, side):
+        src = wt_ref if dist == 1 else held_wt.at[dist - 2, side]
+        dst = far_wt if dist == half else held_wt.at[dist - 1, side]
+        return remote(src, dst, wt_send.at[dist - 1, side], wt_recv.at[dist - 1, side], ahead[side][0])
+
+    hops, tables = {}, {}
+    for dist in range(1, half + 1):
+        for side in range(2):
+            if dist < half or side == 0:
+                tables[dist, side] = table_copy(dist, side)
             for j in range(SUBS):
-                if dist == 1:
-                    src = x_ref.at[:, pl.ds(j * part, part)]
-                else:
-                    src = held.at[dist - 2, j, side_rows(side)]
-                copies.append(remote(src, held.at[dist - 1, j, side_rows(side)],
-                                     ag_send.at[dist - 1, side, j], ag_recv.at[dist - 1, side, j], peer))
-            wsrc = wt_ref if dist == 1 else held_wt.at[dist - 2, side]
-            copies.append(remote(wsrc, held_wt.at[dist - 1, side],
-                                 wt_send.at[dist - 1, side], wt_recv.at[dist - 1, side], peer))
-        return copies
-
-    def far_copies():
-        copies = []
-        for side, peer in ((0, right), (1, left)):
-            for j in range(SUBS):
-                copies.append(remote(held.at[half - 2, j, pl.ds(side * rows + side * mid, mid)],
-                                     far.at[j, pl.ds(side * mid, mid)],
-                                     far_send.at[side, j], far_recv.at[side, j], peer))
-        copies.append(remote(held_wt.at[half - 2, 0], far_wt, wt_send.at[half - 1, 0],
-                             wt_recv.at[half - 1, 0], right))
-        return copies
-
-    hops = [gather_copies(dist) for dist in range(1, half)] + [far_copies()]
-    for copy in hops[0]:
-        copy.start()
+                if dist < half or j == side:
+                    hops[dist, side, j] = hop_copy(dist, side, j)
+    for side in range(2):
+        tables[1, side].start()
+    for j in range(SUBS):
+        for side in range(2):
+            hops[1, side, j].start()
 
     loads = [pltpu.make_async_copy(wg_ref, gates.at[core], load_sem.at[0]),
              pltpu.make_async_copy(wu_ref, ups.at[core], load_sem.at[1]),
@@ -89,12 +94,37 @@
     for copy in loads + swaps:
         copy.start()
 
-    def column(table):
+    def line_of(table, name):
         names = lax.broadcasted_iota(jnp.int32, table.shape, 0)
-        line_of = jnp.sum(jnp.where(names == me, table, 0.0), axis=0, keepdims=True)
+        return jnp.sum(jnp.where(names == name, table, 0.0), axis=0, keepdims=True)
+
+    def column(flat):
         square = (rows, rows)
         same = lax.broadcasted_iota(jnp.int32, square, 0) == lax.broadcasted_iota(jnp.int32, square, 1)
-        return jnp.sum(jnp.where(same, jnp.broadcast_to(line_of, square), 0.0), axis=1, keepdims=True)
+        return jnp.sum(jnp.where(same, jnp.broadcast_to(flat, square), 0.0), axis=1, keepdims=True)
+
+    def chosen_rows(table, owner):
+        slots = jnp.broadcast_to(line_of(table, experts + owner), (cap, rows)).astype(jnp.int32)
+        return slots == lax.broadcasted_iota(jnp.int32, (cap, rows), 0)
+
+    def ones(mask):
+        return jnp.where(mask, 1.0, 0.0).astype(jnp.bfloat16)
+
+    def spread(table, owner):
+        slots = jnp.broadcast_to(column(line_of(table, experts + owner)), (rows, cap)).astype(jnp.int32)
+        return ones(slots == lax.broadcasted_iota(jnp.int32, (rows, cap), 1))
+
+    def narrow(mask, source, target):
+        def one(t, carry):
+            cols = pl.ds(pl.multiple_of(t * units, units), units)
+            target[:, cols] = jnp.dot(mask, source[:, cols], preferred_element_type=jnp.float32).astype(jnp.bfloat16)
+            return carry
+
+        lax.fori_loop(0, part // units, one, 0)
+
+    def narrow_weight(table):
+        picked = chosen_rows(table, me)
+        return jnp.sum(jnp.where(picked, jnp.broadcast_to(line_of(table, me), (cap, rows)), 0.0), axis=1, keepdims=True)
 
     def expand(chunks, weight, target):
         def one(q, carry):
@@ -113,25 +143,49 @@
         lax.fori_loop(0, 2 * units // TILE, one, 0)
 
     for dist in range(1, half):
-        for copy in hops[dist - 1]:
-            copy.wait_recv()
-        for copy in hops[dist]:
-            copy.start()
+        for side in range(2):
+            tables[dist, side].wait_recv()
+            if (dist + 1, side) in tables:
+                tables[dist + 1, side].start()
+        if dist == half - 1:
+            for side in range(2):
+                for j in range(SUBS):
+                    hops[2, side, j].wait_send()
+        for j in range(SUBS):
+            for side in range(2):
+                hops[dist, side, j].wait_recv()
+                if (dist + 1, side, j) not in hops:
+                    continue
+                if dist + 1 == half or (dist + 1 == half - 1 and j != side):
+                    mask = ones(chosen_rows(held_wt[dist - 1, side], ahead[side][1]))
+                    narrow(mask, held.at[dist - 1, j, side_rows(side)],
+                           stage_far.at[side] if dist + 1 == half else stage.at[side])
+                hops[dist + 1, side, j].start()
         if dist == 1:
             for copy in loads:
                 copy.wait()
             for copy in swaps[:2]:
                 copy.wait()
-            expand([own.at[j] for j in range(SUBS)], column(own_wt[...]), hid_own)
-        weight = jnp.concatenate([column(held_wt[dist - 1, 0]), column(held_wt[dist - 1, 1])], axis=0)
-        expand([held.at[dist - 1, j] for j in range(SUBS)], weight, hid.at[dist - 1])
+            expand([own.at[j] for j in range(SUBS)], column(line_of(own_wt[...], me)), hid_own)
+        if dist < half - 1:
+            weight = jnp.concatenate([column(line_of(held_wt[dist - 1, side], me)) for side in range(2)], axis=0)
+            expand([held.at[dist - 1, j] for j in range(SUBS)], weight, hid.at[dist - 1])
+        else:
+            for side in range(2):
+                mask = ones(chosen_rows(held_wt[dist - 1, side], me))
+                narrow(mask, held.at[dist - 1, side, side_rows(side)], late.at[side, cap_rows(side)])
+            weight = jnp.concatenate([narrow_weight(held_wt[dist - 1, side]) for side in range(2)], axis=0)
+            expand([late.at[j] for j in range(SUBS)], weight, hid_late)
     swaps[2].wait()
-    for copy in hops[half - 1]:
-        copy.wait_recv()
-    expand([far.at[j] for j in range(SUBS)], column(far_wt[...]), hid_far)
-    for hop in hops:
-        for copy in hop:
+    tables[half, 0].wait_recv()
+    for side in range(2):
+        hops[half, side, side].wait_recv()
+    expand([far.at[j] for j in range(SUBS)], narrow_weight(far_wt[...]), hid_far)
+    for name, copy in hops.items():
+        if name[0] != 2:
             copy.wait_send()
+    for copy in tables.values():
+        copy.wait_send()
 
     blocks = width // units
 
@@ -163,53 +217,69 @@
 
         lax.fori_loop(0, part // units, one, 0)
 
+    back = ((left, right_owner), (right, left_owner))
     sums = {}
-    for j in range(SUBS):
-        def write(cols, total, j=j):
-            first_out[j, :, cols] = total.astype(jnp.bfloat16)
+
+    def send(k, side, j, src, dst):
+        copy = remote(src, dst, rs_send.at[k, side, j], rs_recv.at[k, side, j], back[side][0])
+        copy.start()
+        sums[k, side, j] = copy
+
+    for j in range(SUBS):
+        side = 1 - j
+
+        def write(cols, total, side=side):
+            stage_far[side, :, cols] = total.astype(jnp.bfloat16)
 
         contract(j, hid_far, write)
-        pair = []
-        for side, peer in ((0, left), (1, right)):
-            piece = pl.ds((1 - side) * mid, mid)
-            pair.append(remote(first_out.at[j, piece], first_in.at[j, piece],
-                               rs_send.at[0, side, j], rs_recv.at[0, side, j], peer))
-        for copy in pair:
-            copy.start()
-        sums[0, j] = pair
-    for k in range(1, half):
+        send(0, side, j, stage_far.at[side], first_in.at[side])
+    for j in range(SUBS):
+        side = j
+
+        def write(cols, total, side=side):
+            stage[side, :, cols] = total.astype(jnp.bfloat16)
+
+        contract(j, hid_late.at[cap_rows(side)], write)
+        send(1, side, j, stage.at[side], late_in.at[side])
+    for j in range(SUBS):
+        side = 1 - j
+        table = held_wt[half - 2, side]
+        theirs = spread(table, back[side][1])
+        hid_own_rows = jnp.dot(spread(table, me), hid_late[cap_rows(side), :], preferred_element_type=jnp.float32)
+        hid_wide[...] = hid_own_rows.astype(jnp.bfloat16)
+        sums[0, side, j].wait_recv()
+
+        def write(cols, total, side=side, theirs=theirs):
+            second_out[side, :, cols] = (
+                total + jnp.dot(theirs, first_in[side, :, cols], preferred_element_type=jnp.float32)).astype(jnp.bfloat16)
+
+        contract(j, hid_wide, write)
+        send(1, side, j, second_out.at[side], held.at[0, j, side_rows(side)])
+    for k in range(2, half):
         dist = half - k
         for j in range(SUBS):
-            for copy in sums[k - 1, j]:
-                copy.wait_recv()
-            if k == 1:
-                source = second_out.at[j]
-
-                def write(cols, total, j=j):
-                    second_out[j, :mid, cols] = total[:mid].astype(jnp.bfloat16)
-                    second_out[j, mid:rows, cols] = (
-                        total[mid:rows] + first_in[j, mid:, cols].astype(jnp.float32)).astype(jnp.bfloat16)
-                    second_out[j, rows:rows + mid, cols] = (
-                        total[rows:rows + mid] + first_in[j, :mid, cols].astype(jnp.float32)).astype(jnp.bfloat16)
-                    second_out[j, rows + mid:, cols] = total[rows + mid:].astype(jnp.bfloat16)
+            for side in range(2):
+                sums[k - 1, side, j].wait_recv()
+            if k == 2:
+                theirs = spread(held_wt[dist - 1, j], back[j][1])
+
+                def write(cols, total, j=j, theirs=theirs):
+                    early, full = slice(j * rows, (j + 1) * rows), slice((1 - j) * rows, (2 - j) * rows)
+                    held[0, j, early, cols] = (total[early] + jnp.dot(
+                        theirs, late_in[j, :, cols], preferred_element_type=jnp.float32)).astype(jnp.bfloat16)
+                    held[0, j, full, cols] = (
+                        total[full] + held[0, j, full, cols].astype(jnp.float32)).astype(jnp.bfloat16)
             else:
-                source = held.at[k - 2, j]
-
                 def write(cols, total, k=k, j=j):
                     held[k - 2, j, :, cols] = (
                         total + held[k - 2, j, :, cols].astype(jnp.float32)).astype(jnp.bfloat16)
 
             contract(j, hid.at[dist - 1], write)
-            pair = []
-            for side, peer in ((0, left), (1, right)):
-                pair.append(remote(source.at[side_rows(side)], held.at[k - 1, j, side_rows(side)],
-                                   rs_send.at[k, side, j], rs_recv.at[k, side, j], peer))
-            for copy in pair:
-                copy.start()
-            sums[k, j] = pair
-    for j in range(SUBS):
-        for copy in sums[half - 1, j]:
-            copy.wait_recv()
+            for side in range(2):
+                send(k, side, j, held.at[k - 2, j, side_rows(side)], held.at[k - 1, j, side_rows(side)])
+    for j in range(SUBS):
+        for side in range(2):
+            sums[half - 1, side, j].wait_recv()
 
         def write(cols, total, j=j):
             both = held[half - 2, j, :rows, cols].astype(jnp.float32) + held[half - 2, j, rows:, cols].astype(jnp.float32)
@@ -217,9 +287,8 @@
 
         contract(j, hid_own, write)
         out_ref[:, j * part:(j + 1) * part] = own[j]
-    for pair in sums.values():
-        for copy in pair:
-            copy.wait_send()
+    for copy in sums.values():
+        copy.wait_send()
 
 
 def ring_shards(tokens, expert_ids, gate_values, w_gate, w_up, w_down):
@@ -228,7 +297,12 @@
     units = w_gate.shape[2]
     half = experts // 2
     chosen = expert_ids.T[:, None, :] == jnp.arange(experts, dtype=jnp.int32)[None, :, None]
-    table = jnp.sum(jnp.where(chosen, gate_values.T[:, None, :], 0.0), axis=0)
+    weight = jnp.sum(jnp.where(chosen, gate_values.T[:, None, :], 0.0), axis=0)
+    named = jnp.any(chosen, axis=0)
+    before = (jnp.arange(rows)[:, None] < jnp.arange(rows)[None, :]).astype(jnp.bfloat16)
+    slots = jnp.dot(named.astype(jnp.bfloat16), before, preferred_element_type=jnp.float32)
+    table = jnp.concatenate([weight, jnp.where(named, slots, -1.0)], axis=0)
+    cap = (rows * expert_ids.shape[1] * 5 // (4 * experts) + 15) // 16 * 16
     part = width // SUBS
     bf, f32 = jnp.bfloat16, jnp.float32
     dma = pltpu.SemaphoreType.DMA
@@ -243,20 +317,24 @@
             pltpu.VMEM((2, width, units), bf),
             pltpu.VMEM((SUBS, rows, part), bf),
             pltpu.VMEM((half - 1, SUBS, 2 * rows, part), bf),
-            pltpu.VMEM((SUBS, rows, part), bf),
-            pltpu.VMEM((experts, rows), f32),
-            pltpu.VMEM((half - 1, 2, experts, rows), f32),
-            pltpu.VMEM((experts, rows), f32),
+            pltpu.VMEM((SUBS, 2 * cap, part), bf),
+            pltpu.VMEM((SUBS, cap, part), bf),
+            pltpu.VMEM((2 * experts, rows), f32),
+            pltpu.VMEM((half - 1, 2, 2 * experts, rows), f32),
+            pltpu.VMEM((2 * experts, rows), f32),
             pltpu.VMEM((rows, 2 * units), bf),
-            pltpu.VMEM((half - 1, 2 * rows, 2 * units), bf),
+            pltpu.VMEM((half - 2, 2 * rows, 2 * units), bf),
+            pltpu.VMEM((2 * cap, 2 * units), bf),
+            pltpu.VMEM((cap, 2 * units), bf),
             pltpu.VMEM((rows, 2 * units), bf),
-            pltpu.VMEM((SUBS, rows, part), bf),
-            pltpu.VMEM((SUBS, rows, part), bf),
-            pltpu.VMEM((SUBS, 2 * rows, part), bf),
+            pltpu.VMEM((2, cap, part), bf),
+            pltpu.VMEM((2, cap, part), bf),
+            pltpu.VMEM((2, cap, part), bf),
+            pltpu.VMEM((2, cap, part), bf),
+            pltpu.VMEM((2, rows, part), bf),
             dma((3 + SUBS,)), dma((3,)), dma((3,)),
-            dma((half - 1, 2, SUBS)), dma((half - 1, 2, SUBS)),
+            dma((half, 2, SUBS)), dma((half, 2, SUBS)),
             dma((half, 2)), dma((half, 2)),
-            dma((2, SUBS)), dma((2, SUBS)),
             dma((half, 2, SUBS)), dma((half, 2, SUBS)),
             dma((2, width // units)),
         ],
@@ -328,7 +406,7 @@
         block = tokens.size * 2 // mesh.size
         weights = w_gate.size * 2 // experts
         need = block * (experts + 7) + 2 * weights
-        fits = cores == 2 and experts % 2 == 0 and experts >= 4 and need <= 58 * 2 ** 20
+        fits = cores == 2 and experts % 2 == 0 and experts >= 8 and need <= 58 * 2 ** 20
         return jax.shard_map(
             ring_shards if fits else shards,
             mesh=mesh,

time: 305 us -> 280 us (0.918)
  Pallas kernels: 301 us -> 275 us
    pallas_call x1, Pallas kernels: 301 us -> 275 us  [ring_shards(): pl.pallas_call(functools.partial(ring_kernel, experts), out_shape=(jax.Sh...]
where the time goes in v3:
time: 280 us
  Pallas kernels  275 us (98%)
  local copies, waits for them, and re-layouts  2.85 us (1%)
    pallas_call x1, Pallas kernels, ring_shards(): pl.pallas_call(functools.partial(ring_kernel, experts), out_shape=(jax.Sh...  275 us

profile of v3, /device:TPU:0, one launch (start us, length us, event | category | flops | bytes accessed | tf_op | source)
XLA Modules:
  0.0 280.1 jit_solution(11720882600118388069)
XLA Ops:
  0.0 0.7 fusion
  0.7 0.1 convolution_select_fusion
  0.8 0.7 select_reduce_fusion
  1.5 0.6 pad_maximum_fusion.wt_ref
  2.1 275.2 %shard_map.64 = (bf16[128,7168]{1,0:T(8,128)(2,1)}, bf16[512,7168]{1,0:T(8,128)(2,1)}) custom-call(bf16[128,7168]{1,0:T(8,128)(2,1)} %x_ref.1, f32[16,128]{1,0:T(8,128)} %pad_maximum_fusion.wt_ref, bf16[7168,512]{1,0:T(8,128)(2,1)} %bitcast.6, bf16[7168,512]{1,0:T(8,128)(2,1)} %bitcast.7, bf16[512,7168]{1,0:T(8,128)(2,1)} %bitcast.8), custom_call_target="tpu_custom_call" | custom-call | tf_op jit(solution)/shard_map/pallas_call | solution.py:310
  277.3 2.8 %copy.8 = bf16[128,7168]{1,0:T(8,128)(2,1)} copy(bf16[128,7168]{1,0:T(8,128)(2,1)} %get-tuple-element.6) | data formatting | bytes 3670016

commit v4 on v3

--- a/solution.py
+++ b/solution.py
@@ -13,9 +13,9 @@
 
 def ring_kernel(experts, x_ref, wt_ref, wg_ref, wu_ref, wd_ref, out_ref, sib_ref,
                 gates, ups, own, held, late, far, own_wt, held_wt, far_wt,
-                hid_own, hid, hid_late, hid_far, hid_wide, stage, stage_far, first_in, late_in, second_out,
+                hid_own, hid, hid_late, hid_far, hid_wide, stage, stage_far, first_in, late_in, second_out, tiles,
                 load_sem, sib_send, sib_recv, ag_send, ag_recv, wt_send, wt_recv,
-                rs_send, rs_recv, down_sem):
+                rs_send, rs_recv, down_sem, tile_sem):
     half = experts // 2
     rows, width = x_ref.shape
     units = wg_ref.shape[1]
@@ -177,12 +177,53 @@
             weight = jnp.concatenate([narrow_weight(held_wt[dist - 1, side]) for side in range(2)], axis=0)
             expand([late.at[j] for j in range(SUBS)], weight, hid_late)
     swaps[2].wait()
+
+    back = ((left, right_owner), (right, left_owner))
+    sums = {}
+
+    def send(k, side, j, src, dst):
+        copy = remote(src, dst, rs_send.at[k, side, j], rs_recv.at[k, side, j], back[side][0])
+        copy.start()
+        sums[k, side, j] = copy
+
+    per_part = part // units
+
+    def tile_copies(b, slot):
+        place = pl.ds(pl.multiple_of(b * units, units), units)
+        return [pltpu.make_async_copy(wd_ref.at[:, place], tiles.at[slot, core], tile_sem.at[slot, 0]),
+                pltpu.make_async_copy(sib_ref.at[:, place], tiles.at[slot, 1 - core], tile_sem.at[slot, 1])]
+
+    for side in range(2):
+        for j in range(SUBS):
+            if j != side:
+                hops[half - 1, side, j].wait_send()
+    for copy in tile_copies(0, 0):
+        copy.start()
+    for j in range(SUBS):
+        def late_one(t, carry, j=j):
+            b = j * per_part + t
+            slot = b % 2
+
+            @pl.when(b + 1 < SUBS * per_part)
+            def _():
+                for copy in tile_copies(b + 1, 1 - slot):
+                    copy.start()
+
+            for copy in tile_copies(b, slot):
+                copy.wait()
+            total = jnp.dot(hid_late[cap_rows(j), :units], tiles[slot, 0], preferred_element_type=jnp.float32)
+            total += jnp.dot(hid_late[cap_rows(j), units:], tiles[slot, 1], preferred_element_type=jnp.float32)
+            stage[j, :, pl.ds(pl.multiple_of(t * units, units), units)] = total.astype(jnp.bfloat16)
+            return carry
+
+        lax.fori_loop(0, per_part, late_one, 0)
+        send(1, j, j, stage.at[j], late_in.at[j])
     tables[half, 0].wait_recv()
     for side in range(2):
         hops[half, side, side].wait_recv()
     expand([far.at[j] for j in range(SUBS)], narrow_weight(far_wt[...]), hid_far)
     for name, copy in hops.items():
-        if name[0] != 2:
+        if name[0] != 2 and not (name[0] == half - 1 and name[1] != name[2]):
             copy.wait_send()
     for copy in tables.values():
         copy.wait_send()
@@ -205,8 +246,6 @@
         return carry
 
     lax.fori_loop(0, blocks, start_down, 0)
-    lax.fori_loop(0, blocks, wait_down, 0)
-
     def contract(j, hidden, write):
         def one(t, carry):
             place = pl.ds(pl.multiple_of((j * (part // units) + t) * units, units), units)
@@ -217,30 +256,15 @@
 
         lax.fori_loop(0, part // units, one, 0)
 
-    back = ((left, right_owner), (right, left_owner))
-    sums = {}
-
-    def send(k, side, j, src, dst):
-        copy = remote(src, dst, rs_send.at[k, side, j], rs_recv.at[k, side, j], back[side][0])
-        copy.start()
-        sums[k, side, j] = copy
-
     for j in range(SUBS):
         side = 1 - j
 
         def write(cols, total, side=side):
             stage_far[side, :, cols] = total.astype(jnp.bfloat16)
 
+        lax.fori_loop(j * per_part, (j + 1) * per_part, wait_down, 0)
         contract(j, hid_far, write)
         send(0, side, j, stage_far.at[side], first_in.at[side])
-    for j in range(SUBS):
-        side = j
-
-        def write(cols, total, side=side):
-            stage[side, :, cols] = total.astype(jnp.bfloat16)
-
-        contract(j, hid_late.at[cap_rows(side)], write)
-        send(1, side, j, stage.at[side], late_in.at[side])
     for j in range(SUBS):
         side = 1 - j
         table = held_wt[half - 2, side]
@@ -332,11 +356,12 @@
             pltpu.VMEM((2, cap, part), bf),
             pltpu.VMEM((2, cap, part), bf),
             pltpu.VMEM((2, rows, part), bf),
+            pltpu.VMEM((2, 2, units, units), bf),
             dma((3 + SUBS,)), dma((3,)), dma((3,)),
             dma((half, 2, SUBS)), dma((half, 2, SUBS)),
             dma((half, 2)), dma((half, 2)),
             dma((half, 2, SUBS)), dma((half, 2, SUBS)),
-            dma((2, width // units)),
+            dma((2, width // units)), dma((2, 2)),
         ],
         compiler_params=pltpu.CompilerParams(
             collective_id=0, has_side_effects=True, vmem_limit_bytes=60 * 2 ** 20),

time: 280 us -> 279 us (level)
  no operation moved by 1% of the time
where the time goes in v4:
time: 279 us
  Pallas kernels  274 us (98%)
  local copies, waits for them, and re-layouts  2.85 us (1%)
    pallas_call x1, Pallas kernels, ring_shards(): pl.pallas_call(functools.partial(ring_kernel, experts), out_shape=(jax.Sh...  274 us

profile of v4, /device:TPU:0, one launch (start us, length us, event | category | flops | bytes accessed | tf_op | source)
XLA Modules:
  0.0 278.5 jit_solution(11494836427540713353)
XLA Ops:
  0.0 0.7 fusion
  0.7 0.1 convolution_select_fusion
  0.8 0.7 select_reduce_fusion
  1.5 0.6 pad_maximum_fusion.wt_ref
  2.1 273.5 %shard_map.64 = (bf16[128,7168]{1,0:T(8,128)(2,1)}, bf16[512,7168]{1,0:T(8,128)(2,1)}) custom-call(bf16[128,7168]{1,0:T(8,128)(2,1)} %x_ref.1, f32[16,128]{1,0:T(8,128)} %pad_maximum_fusion.wt_ref, bf16[7168,512]{1,0:T(8,128)(2,1)} %bitcast.6, bf16[7168,512]{1,0:T(8,128)(2,1)} %bitcast.7, bf16[512,7168]{1,0:T(8,128)(2,1)} %bitcast.8), custom_call_target="tpu_custom_call" | custom-call | tf_op jit(solution)/shard_map/pallas_call | solution.py:334
  275.7 2.8 %copy.8 = bf16[128,7168]{1,0:T(8,128)(2,1)} copy(bf16[128,7168]{1,0:T(8,128)(2,1)} %get-tuple-element.6) | data formatting | bytes 3670016
